TPU v7x, 128 devices: a whole 4x4x4 slice. The times are simulated.
128 devices in a mesh: ctx: 32 (over x, y, z_hi), wsh: 4 (over z_lo, core).
Axes of the slice: x: 4, y: 4, z: 4 (z_hi: 2, z_lo: 2; z = z_hi * 2 + z_lo), core: 2. Of those that a mesh axis runs over, the one named last changes fastest.
Arguments:
- tokens: bfloat16 [4, 4096, 1024], P('wsh', 'ctx'), may hold values from -6 to 6
- places: int32 [4, 4096], P('wsh', 'ctx'), may hold values from 0 to 4095, as said below
- w_qkv: bfloat16 [1024, 3072], P('wsh'), may hold values from -0.1875 to 0.1875
- b_qv: bfloat16 [2048], P('wsh'), may hold values from -3 to 3
- w_out: bfloat16 [1024, 1024], P('wsh'), may hold values from -0.5 to 0.5
- b_out: bfloat16 [1024], P('wsh'), may hold values from -3 to 3
- norm1_gain: bfloat16 [1024], P('wsh'), may hold values from 0.5 to 1.5
- norm1_shift: bfloat16 [1024], P('wsh'), may hold values from -3 to 3
- norm2_gain: bfloat16 [1024], P('wsh'), may hold values from 0.5 to 1.5
- norm2_shift: bfloat16 [1024], P('wsh'), may hold values from -3 to 3
- w_up: bfloat16 [1024, 4096], P('wsh'), may hold values from -0.1875 to 0.1875
- b_up: bfloat16 [4096], P('wsh'), may hold values from -3 to 3
- w_down: bfloat16 [4096, 1024], P('wsh'), may hold values from -0.09375 to 0.09375
- b_down: bfloat16 [1024], P('wsh'), may hold values from -3 to 3
- cotangent: bfloat16 [4, 4096, 1024], P('wsh', 'ctx'), may hold values from -6 to 6
Outputs:
- output: bfloat16 [4, 4096, 1024], P('wsh', 'ctx')
- grad_tokens: bfloat16 [4, 4096, 1024], P('wsh', 'ctx')
- grad_w_qkv: float32 [1024, 3072], P('wsh')
- grad_b_qv: float32 [2048], P('wsh')
- grad_w_out: float32 [1024, 1024], P('wsh')
- grad_b_out: float32 [1024], P('wsh')
- grad_norm1_gain: float32 [1024], P('wsh')
- grad_norm1_shift: float32 [1024], P('wsh')
- grad_norm2_gain: float32 [1024], P('wsh')
- grad_norm2_shift: float32 [1024], P('wsh')
- grad_w_up: float32 [1024, 4096], P('wsh')
- grad_b_up: float32 [4096], P('wsh')
- grad_w_down: float32 [4096, 1024], P('wsh')
- grad_b_down: float32 [1024], P('wsh')
Inputs may be any that keep to these rules, and one draw needn't show every extreme that they name: `places`: within each sequence every position appears once; each device's 128 stored tokens along ctx are two runs of 64 consecutive positions, the run starting at b * 64 followed by the run starting at 4096 - (b + 1) * 64, with b different on every device of the sequence.
All inputs are finite; a program needn't handle non-finite values.
Results may differ from a plain program's by a relative error of at most 0.04.
Values may be sent and summed in bfloat16 or wider, within the bound.
No kernel may reach another device: no remote copies, remote signals or barrier semaphores. Data moves between devices by JAX's collectives and lax.ppermute only.
A program may use at most 192 MiB of HBM per device.

v0:
```python
import jax
import jax.numpy as jnp
from jax import lax
from jax.sharding import PartitionSpec as P

HEADS = 16
HEAD_DIM = 64


EPS = 1e-05
BLOCK = 512
NEGATIVE = -1e30


def layer_norm(values, gain_vec, shift_vec):
    average = jnp.mean(values, axis=-1, keepdims=True)
    centred = values - average
    variance = jnp.mean(centred * centred, axis=-1, keepdims=True)
    return centred * lax.rsqrt(variance + EPS) * gain_vec + shift_vec


def gelu_tanh(values):
    return (
        0.5
        * values
        * (1.0 + jnp.tanh(0.7978845608028654 * (values + 0.044715 * values * values * values)))
    )


def contract_rows(left, right):
    return lax.dot_general(
        left, right, (((0,), (0,)), ((), ())), preferred_element_type=jnp.float32
    )


def contract_cols(left, right):
    return lax.dot_general(
        left, right, (((1,), (1,)), ((), ())), preferred_element_type=jnp.float32
    )


def alibi_scores(query, keys, query_places, key_places, slopes):
    key_rows = keys.shape[0]
    k_heads = keys.reshape(key_rows, HEADS, HEAD_DIM)
    scores = jnp.einsum(
        "qhd,khd->hqk", query, k_heads, preferred_element_type=jnp.float32
    ) * HEAD_DIM ** (-0.5)
    distance = (query_places[:, None] - key_places[None, :]).astype(jnp.float32)
    allowed = (key_places[None, :] <= query_places[:, None])[None, :, :]
    return (scores - slopes[:, None, None] * distance[None, :, :], allowed, k_heads)


def fold_block(carry, query, keys, values, query_places, key_places, slopes):
    highest, total, accum = carry
    scores, allowed, k_heads = alibi_scores(query, keys, query_places, key_places, slopes)
    v_heads = values.reshape(keys.shape[0], HEADS, HEAD_DIM)
    block_high = jnp.max(jnp.where(allowed, scores, NEGATIVE), axis=-1)
    new_high = jnp.maximum(highest, block_high)
    weights = jnp.where(allowed, jnp.exp(scores - new_high[:, :, None]), 0.0)
    factor = jnp.exp(highest - new_high)
    total = total * factor + jnp.sum(weights, axis=-1)
    accum = accum * factor.T[:, :, None] + jnp.einsum(
        "hqk,khd->qhd", weights.astype(jnp.bfloat16), v_heads, preferred_element_type=jnp.float32
    )
    return (new_high, total, accum)


def fold_rows(carry, query, keys, values, query_places, key_places, slopes):
    key_rows = keys.shape[0]
    count_blocks = key_rows // BLOCK

    def fold_step(state, inputs):
        return (
            fold_block(state, query, inputs[0], inputs[1], query_places, inputs[2], slopes),
            None,
        )

    carry, unused = lax.scan(
        fold_step,
        carry,
        (
            keys.reshape(count_blocks, BLOCK, -1),
            values.reshape(count_blocks, BLOCK, -1),
            key_places.reshape(count_blocks, BLOCK),
        ),
    )
    return carry


def unfold_scores(
    query, d_out, log_rows, delta_rows, keys, values, query_places, key_places, slopes
):
    scores, allowed, k_heads = alibi_scores(query, keys, query_places, key_places, slopes)
    v_heads = values.reshape(keys.shape[0], HEADS, HEAD_DIM)
    weights = jnp.where(allowed, jnp.exp(scores - log_rows.T[:, :, None]), 0.0)
    d_weights = jnp.einsum("qhd,khd->hqk", d_out, v_heads, preferred_element_type=jnp.float32)
    d_scores = (weights * (d_weights - delta_rows.T[:, :, None])).astype(jnp.bfloat16)
    return (weights, d_scores, k_heads)


def key_value_terms(weights, d_scores, query, d_out):
    key_rows = d_scores.shape[2]
    grad_keys = jnp.einsum(
        "hqk,qhd->khd", d_scores, query, preferred_element_type=jnp.float32
    ) * HEAD_DIM ** (-0.5)
    grad_values = jnp.einsum(
        "hqk,qhd->khd", weights.astype(jnp.bfloat16), d_out, preferred_element_type=jnp.float32
    )
    return jnp.concatenate(
        [grad_keys.reshape(key_rows, -1), grad_values.reshape(key_rows, -1)], axis=1
    )


def unfold_block(
    grad_query, query, d_out, log_rows, delta_rows, keys, values, query_places, key_places, slopes
):
    weights, d_scores, k_heads = unfold_scores(
        query, d_out, log_rows, delta_rows, keys, values, query_places, key_places, slopes
    )
    grad_query = grad_query + jnp.einsum(
        "hqk,khd->qhd", d_scores, k_heads, preferred_element_type=jnp.float32
    ) * HEAD_DIM ** (-0.5)
    return (grad_query, key_value_terms(weights, d_scores, query, d_out))


def body(
    tokens,
    places,
    w_qkv,
    b_qv,
    w_out,
    b_out,
    norm1_gain,
    norm1_shift,
    norm2_gain,
    norm2_shift,
    w_up,
    b_up,
    w_down,
    b_down,
    cotangent,
):
    (
        full_qkv,
        full_bqv,
        full_out,
        full_bout,
        gain_one,
        shift_one,
        gain_two,
        shift_two,
        full_up,
        full_bup,
        full_down,
        full_bdown,
    ) = (
        lax.all_gather(w_qkv, "wsh", axis=0, tiled=True),
        lax.all_gather(b_qv, "wsh", axis=0, tiled=True),
        lax.all_gather(w_out, "wsh", axis=0, tiled=True),
        lax.all_gather(b_out, "wsh", axis=0, tiled=True),
        lax.all_gather(norm1_gain, "wsh", axis=0, tiled=True),
        lax.all_gather(norm1_shift, "wsh", axis=0, tiled=True),
        lax.all_gather(norm2_gain, "wsh", axis=0, tiled=True),
        lax.all_gather(norm2_shift, "wsh", axis=0, tiled=True),
        lax.all_gather(w_up, "wsh", axis=0, tiled=True),
        lax.all_gather(b_up, "wsh", axis=0, tiled=True),
        lax.all_gather(w_down, "wsh", axis=0, tiled=True),
        lax.all_gather(b_down, "wsh", axis=0, tiled=True),
    )
    width = HEADS * HEAD_DIM
    rows = tokens.shape[1]
    seq_length = rows * lax.axis_size("ctx")
    slopes = (
        8.0 * jnp.exp2(-4.0 * (jnp.arange(HEADS, dtype=jnp.float32) + 1.0) / HEADS) / seq_length
    )
    residual_in = tokens[0].astype(jnp.float32)
    query_places = places[0]
    key_places = lax.all_gather(query_places, "ctx", axis=0, tiled=True)
    normed_one, norm_one_back = jax.vjp(
        layer_norm, residual_in, gain_one.astype(jnp.float32), shift_one.astype(jnp.float32)
    )
    normed_one = normed_one.astype(jnp.bfloat16)
    mixed = jnp.dot(normed_one, full_qkv, preferred_element_type=jnp.float32)
    bias_qv = full_bqv.astype(jnp.float32)
    query = (mixed[:, :width] + bias_qv[:width]).astype(jnp.bfloat16)
    keys = mixed[:, width : 2 * width].astype(jnp.bfloat16)
    values = (mixed[:, 2 * width :] + bias_qv[width:]).astype(jnp.bfloat16)
    query_heads = query.reshape(rows, HEADS, HEAD_DIM)
    start_state = (
        jnp.full((HEADS, rows), NEGATIVE, jnp.float32),
        jnp.zeros((HEADS, rows), jnp.float32),
        jnp.zeros((rows, HEADS, HEAD_DIM), jnp.float32),
    )
    state = fold_rows(
        start_state,
        query_heads,
        lax.all_gather(keys, "ctx", axis=0, tiled=True),
        lax.all_gather(values, "ctx", axis=0, tiled=True),
        query_places,
        key_places,
        slopes,
    )
    highest, total, accum = state
    log_rows = (highest + jnp.log(total)).T
    out_exact = accum / total.T[:, :, None]
    attended = out_exact.reshape(rows, width).astype(jnp.bfloat16)
    middle = (
        residual_in
        + jnp.dot(attended, full_out, preferred_element_type=jnp.float32)
        + full_bout.astype(jnp.float32)
    )
    normed_two, norm_two_back = jax.vjp(
        layer_norm, middle, gain_two.astype(jnp.float32), shift_two.astype(jnp.float32)
    )
    normed_two = normed_two.astype(jnp.bfloat16)
    pre_act = jnp.dot(normed_two, full_up, preferred_element_type=jnp.float32) + full_bup.astype(
        jnp.float32
    )
    hidden, gelu_back = jax.vjp(gelu_tanh, pre_act)
    hidden = hidden.astype(jnp.bfloat16)
    output = (
        middle
        + jnp.dot(hidden, full_down, preferred_element_type=jnp.float32)
        + full_bdown.astype(jnp.float32)
    )
    d_output = cotangent[0].astype(jnp.float32)
    d_down = d_output.astype(jnp.bfloat16)
    grad_wdown = contract_rows(hidden, d_down)
    grad_bdown = jnp.sum(d_down.astype(jnp.float32), axis=0)
    (d_pre,) = gelu_back(contract_cols(d_down, full_down))
    d_pre = d_pre.astype(jnp.bfloat16)
    grad_wup = contract_rows(normed_two, d_pre)
    grad_bup = jnp.sum(d_pre.astype(jnp.float32), axis=0)
    d_norm_two, grad_gain_two, grad_shift_two = norm_two_back(contract_cols(d_pre, full_up))
    d_middle = d_output + d_norm_two
    d_branch = d_middle.astype(jnp.bfloat16)
    grad_wout = contract_rows(attended, d_branch)
    grad_bout = jnp.sum(d_branch.astype(jnp.float32), axis=0)
    d_attended_flat = contract_cols(d_branch, full_out).astype(jnp.bfloat16)
    d_attended = d_attended_flat.reshape(rows, HEADS, HEAD_DIM)
    delta_rows = jnp.sum(d_attended.astype(jnp.float32) * out_exact, axis=-1)
    keys_back, values_back = (
        lax.all_gather(keys, "ctx", axis=0, tiled=True),
        lax.all_gather(values, "ctx", axis=0, tiled=True),
    )
    total_rows = keys_back.shape[0]
    block = min(BLOCK, total_rows)
    count_blocks = total_rows // block
    back_inputs = (
        keys_back.reshape(count_blocks, block, width),
        values_back.reshape(count_blocks, block, width),
        key_places.reshape(count_blocks, block),
    )
    empty_query = jnp.zeros((rows, HEADS, HEAD_DIM), jnp.float32)

    def back_step(grad_query, inputs):
        return unfold_block(
            grad_query,
            query_heads,
            d_attended,
            log_rows,
            delta_rows,
            inputs[0],
            inputs[1],
            query_places,
            inputs[2],
            slopes,
        )

    grad_query, kv_terms = lax.scan(back_step, empty_query, back_inputs)
    kv_grads = lax.psum_scatter(
        kv_terms.reshape(total_rows, 2 * width).astype(jnp.bfloat16),
        "ctx",
        scatter_dimension=0,
        tiled=True,
    ).astype(jnp.float32)
    d_mixed = jnp.concatenate([grad_query.reshape(rows, width), kv_grads], axis=1).astype(
        jnp.bfloat16
    )
    d_mixed_f32 = d_mixed.astype(jnp.float32)
    grad_wqkv = contract_rows(normed_one, d_mixed)
    grad_bqv = jnp.concatenate(
        [jnp.sum(d_mixed_f32[:, :width], axis=0), jnp.sum(d_mixed_f32[:, 2 * width :], axis=0)]
    )
    d_norm_one, grad_gain_one, grad_shift_one = norm_one_back(contract_cols(d_mixed, full_qkv))
    grad_input = d_middle + d_norm_one
    shares = (
        lax.psum_scatter(
            grad_wqkv.astype(jnp.bfloat16), "wsh", scatter_dimension=0, tiled=True
        ).astype(jnp.float32),
        lax.psum_scatter(
            grad_bqv.astype(jnp.bfloat16), "wsh", scatter_dimension=0, tiled=True
        ).astype(jnp.float32),
        lax.psum_scatter(
            grad_wout.astype(jnp.bfloat16), "wsh", scatter_dimension=0, tiled=True
        ).astype(jnp.float32),
        lax.psum_scatter(
            grad_bout.astype(jnp.bfloat16), "wsh", scatter_dimension=0, tiled=True
        ).astype(jnp.float32),
        lax.psum_scatter(
            grad_gain_one.astype(jnp.bfloat16), "wsh", scatter_dimension=0, tiled=True
        ).astype(jnp.float32),
        lax.psum_scatter(
            grad_shift_one.astype(jnp.bfloat16), "wsh", scatter_dimension=0, tiled=True
        ).astype(jnp.float32),
        lax.psum_scatter(
            grad_gain_two.astype(jnp.bfloat16), "wsh", scatter_dimension=0, tiled=True
        ).astype(jnp.float32),
        lax.psum_scatter(
            grad_shift_two.astype(jnp.bfloat16), "wsh", scatter_dimension=0, tiled=True
        ).astype(jnp.float32),
        lax.psum_scatter(
            grad_wup.astype(jnp.bfloat16), "wsh", scatter_dimension=0, tiled=True
        ).astype(jnp.float32),
        lax.psum_scatter(
            grad_bup.astype(jnp.bfloat16), "wsh", scatter_dimension=0, tiled=True
        ).astype(jnp.float32),
        lax.psum_scatter(
            grad_wdown.astype(jnp.bfloat16), "wsh", scatter_dimension=0, tiled=True
        ).astype(jnp.float32),
        lax.psum_scatter(
            grad_bdown.astype(jnp.bfloat16), "wsh", scatter_dimension=0, tiled=True
        ).astype(jnp.float32),
    )
    shares = (
        lax.psum(shares[0].astype(jnp.bfloat16), "ctx").astype(jnp.float32),
        lax.psum(shares[1].astype(jnp.bfloat16), "ctx").astype(jnp.float32),
        lax.psum(shares[2].astype(jnp.bfloat16), "ctx").astype(jnp.float32),
        lax.psum(shares[3].astype(jnp.bfloat16), "ctx").astype(jnp.float32),
        lax.psum(shares[4].astype(jnp.bfloat16), "ctx").astype(jnp.float32),
        lax.psum(shares[5].astype(jnp.bfloat16), "ctx").astype(jnp.float32),
        lax.psum(shares[6].astype(jnp.bfloat16), "ctx").astype(jnp.float32),
        lax.psum(shares[7].astype(jnp.bfloat16), "ctx").astype(jnp.float32),
        lax.psum(shares[8].astype(jnp.bfloat16), "ctx").astype(jnp.float32),
        lax.psum(shares[9].astype(jnp.bfloat16), "ctx").astype(jnp.float32),
        lax.psum(shares[10].astype(jnp.bfloat16), "ctx").astype(jnp.float32),
        lax.psum(shares[11].astype(jnp.bfloat16), "ctx").astype(jnp.float32),
    )
    return (
        output.astype(jnp.bfloat16)[None],
        grad_input.astype(jnp.bfloat16)[None],
        shares[0],
        shares[1],
        shares[2],
        shares[3],
        shares[4],
        shares[5],
        shares[6],
        shares[7],
        shares[8],
        shares[9],
        shares[10],
        shares[11],
    )


def solution(mesh):
    return jax.shard_map(
        body,
        mesh=mesh,
        in_specs=(
            P("wsh", "ctx", None),
            P("wsh", "ctx"),
            P("wsh", None),
            P("wsh"),
            P("wsh", None),
            P("wsh"),
            P("wsh"),
            P("wsh"),
            P("wsh"),
            P("wsh"),
            P("wsh", None),
            P("wsh"),
            P("wsh", None),
            P("wsh"),
            P("wsh", "ctx", None),
        ),
        out_specs=(
            P("wsh", "ctx", None),
            P("wsh", "ctx", None),
            P("wsh", None),
            P("wsh"),
            P("wsh", None),
            P("wsh"),
            P("wsh"),
            P("wsh"),
            P("wsh"),
            P("wsh"),
            P("wsh", None),
            P("wsh"),
            P("wsh", None),
            P("wsh"),
        ),
        check_vma=False,
    )
```

profile of v0, /device:TPU:0, one launch (start us, length us, event | category | flops | bytes accessed | tf_op | source)
XLA Modules:
  0.0 1674.5 jit_solution(11379812563213686397)
XLA Ops:
  8.6 5.1 all-gather.2
  14.3 5.3 all-gather.1
  22.5 52.8 %all-gather.15.cloned.1.call-done = bf16[1024,3072]{1,0:T(8,128)(2,1)} async-done(((bf16[256,3072]{1,0:T(8,128)(2,1)}), bf16[1024,3072]{1,0:T(8,128)(2,1)}) %all-gather.15.cloned.1.call-update) | async-done | bytes 6291472 | tf_op jit(solution)/shard_map/all_gather | solution.py:157
  80.2 5.2 all-gather.3
  88.1 5.1 all-gather.4
  93.2 94.1 %all-gather = s32[1,4096]{1,0:T(1,128)S(1)} all-gather(s32[1,128]{1,0:T(1,128)S(1)} %copy-done.33), channel_id=2, replica_groups=mesh['ctx'=32,'wsh'=4] {'ctx'}, dimensions={1}, use_global_device_ids=true | all-gather | bytes 16896 | tf_op jit(solution)/shard_map/all_gather | solution.py:178
  188.5 5.2 all_gather.59
  193.7 5.1 all-gather.6
  198.8 5.1 all-gather.5
  204.0 11.4 copy.71
  215.5 78.2 %all-gather.19.cloned.1.call-done = bf16[4096,1024]{1,0:T(8,128)(2,1)} async-done(((bf16[128,1024]{1,0:T(8,128)(2,1)}), bf16[4096,1024]{1,0:T(8,128)(2,1)}) %all-gather.19.cloned.1.call-update) | async-done | bytes 8388624 | tf_op jit(solution)/shard_map/all_gather | solution.py:198
  293.7 11.5 copy.72
  305.2 99.7 %while.28 = (s32[]{:T(128)}, f32[16,128]{1,0:T(8,128)S(1)}, f32[16,128]{1,0:T(8,128)S(1)}, f32[128,16,64]{0,2,1:T(8,128)}, s32[8,512]{1,0:T(8,128)S(1)}, /*index...) while((s32[]{:T(128)}, f32[16,128]{1,0:T(8,128)S(1)}, ...), condition=%wide.region_5.6_spmd.clone, body=%wide.region_2.5_spmd.clone.sunk | while | flops 286863424 | bytes 38413732 | solution.py:78
  334.5 4.2 fusion.134
  408.6 4.8 convolution_add_fusion
  413.4 75.2 %all-gather.25.cloned.1.call-done = bf16[4096,1024]{1,0:T(8,128)(2,1)} async-done(((bf16[1024,1024]{1,0:T(8,128)(2,1)}), bf16[4096,1024]{1,0:T(8,128)(2,1)}) %all-gather.25.cloned.1.call-update) | async-done | bytes 8388624 | tf_op jit(solution)/shard_map/all_gather | solution.py:167
  488.6 7.7 fusion.79
  503.5 142.1 %while.29 = (s32[]{:T(128)}, f32[128,16,64]{0,2,1:T(8,128)}, bf16[8,512,2048]{2,1,0:T(8,128)(2,1)}, bf16[8,512,1024]{1,2,0:T(8,128)(2,1)}, s32[8,512]{1,0:T(8,12...) while((s32[]{:T(128)}, f32[128,16,64]{0,2,1:T(8,128)}, ...), condition=%wide.region_12.13_spmd.clone, body=%wide.region_11.12_spmd.clone.sunk | while | flops 691601472 | bytes 78611888 | solution.py:270
  648.7 5.7 convolution_convert_fusion.1
  656.0 5.6 convolution_convert_fusion
  664.5 346.0 %reduce-scatter.6.cloned.1.call-done = bf16[128,2048]{1,0:T(8,128)(2,1)} async-done(((bf16[4096,2048]{1,0:T(8,128)(2,1)}), bf16[128,2048]{1,0:T(8,128)(2,1)}) %reduce-scatter.6.cloned.1.call-update) | async-done | bytes 524304 | tf_op jit(solution)/shard_map/reduce_scatter | solution.py:271
  1010.5 5.6 convolution_convert_fusion.2
  1016.2 25.9 %reduce-scatter.10.cloned.1.call-done = bf16[256,1024]{1,0:T(8,128)(2,1)} async-done(((bf16[1024,1024]{1,0:T(8,128)(2,1)}), bf16[256,1024]{1,0:T(8,128)(2,1)}) %reduce-scatter.10.cloned.1.call-update) | async-done | bytes 524304 | tf_op jit(solution)/shard_map/reduce_scatter | solution.py:294
  1042.1 82.7 %reduce-scatter.12.cloned.1.call-done = bf16[256,4096]{1,0:T(8,128)(2,1)} async-done(((bf16[1024,4096]{1,0:T(8,128)(2,1)}), bf16[256,4096]{1,0:T(8,128)(2,1)}) %reduce-scatter.12.cloned.1.call-update) | async-done | bytes 2097168 | tf_op jit(solution)/shard_map/reduce_scatter | solution.py:312
  1124.8 82.6 %reduce-scatter.14.cloned.1.call-done = bf16[1024,1024]{1,0:T(8,128)(2,1)} async-done(((bf16[4096,1024]{1,0:T(8,128)(2,1)}), bf16[1024,1024]{1,0:T(8,128)(2,1)}) %reduce-scatter.14.cloned.1.call-update) | async-done | bytes 2097168 | tf_op jit(solution)/shard_map/reduce_scatter | solution.py:318
  1207.4 66.1 %reduce-scatter.8.cloned.1.call-done = bf16[256,3072]{1,0:T(8,128)(2,1)} async-done(((bf16[1024,3072]{1,0:T(8,128)(2,1)}), bf16[256,3072]{1,0:T(8,128)(2,1)}) %reduce-scatter.8.cloned.1.call-update) | async-done | bytes 1572880 | tf_op jit(solution)/shard_map/reduce_scatter | solution.py:288
  1274.1 5.1 all-gather.7
  1281.8 5.7 fusion.40
  1287.7 5.2 fusion.73
  1293.3 12.7 all-reduce.10
  1306.5 96.4 %all-reduce.8 = (bf16[512]{0:T(512)(128)(2,1)S(1)}, bf16[256]{0:T(256)(128)(2,1)S(1)}, bf16[256]{0:T(256)(128)(2,1)S(1)}, bf16[256]{0:T(256)(128)(2,1)S(1)}, bf1...) all-reduce(bf16[512]{0:T(512)(128)(2,1)S(1)} %dynamic-slice.1, ...), channel_id=1, replica_groups=mesh['ctx'=32,'wsh'=4] {'ctx'}, use_global_device_ids=true, to_apply=%region_21.22 | all-reduce | flops 3072 | bytes 12288 | tf_op jit(solution)/shard_map/psum | solution.py:327
  1408.5 249.0 %all-reduce.13.cloned.1.call-done = (bf16[256,3072]{1,0:T(8,128)(2,1)}, bf16[256,1024]{1,0:T(8,128)(2,1)}, bf16[256,4096]{1,0:T(8,128)(2,1)}, bf16[1024,1024]{1,0:T(8,128)(2,1)}) async-done(((bf16[256,3072]{1,0:T(8,128)(2,1)}, bf16[256,1024]{1,0:T(8,128)(2,1)}, bf16[256,4096]{1,0:T(8,128)(2,1)}, bf16[1024,1024]{1,0:T(8,128)(2,1)}), (bf16[256,3072]{1,0:T(8,128)(2,1)}, bf16[256,1024]{1,0:T(8,128)(2,1)}, ...) | async-done | bytes 6291472 | tf_op jit(solution)/shard_map/psum | solution.py:326
  (445 shorter events, 285.6 us)
Async XLA Ops:
  7.2 68.1 %all-gather.15.cloned.1.call-start = ((), (), s32[]{:S(2)}) async-start(), calls=%async_computation.5 | async-start | bytes 7864320 | tf_op jit(solution)/shard_map/all_gather | solution.py:157
  7.9 196.1 %all-gather.17.cloned.1.call-start = ((), (), s32[]{:S(2)}) async-start(), calls=%async_computation.6 | async-start | bytes 8650752 | tf_op jit(solution)/shard_map/all_gather | solution.py:197
  13.7 65.6 %copy-start.31 = (f32[4,1,256]{2,1,0:T(1,128)}, f32[4,1,256]{2,1,0:T(1,128)S(1)}, u32[]{:S(2)}) copy-start(f32[4,1,256]{2,1,0:T(1,128)S(1)} %convert_element_type.247) | copy-start | bytes 12292
  19.7 59.6 %copy-start.29 = (f32[4,1,256]{2,1,0:T(1,128)}, f32[4,1,256]{2,1,0:T(1,128)S(1)}, u32[]{:S(2)}) copy-start(f32[4,1,256]{2,1,0:T(1,128)S(1)} %convert_element_type.246) | copy-start | bytes 12292
  20.8 58.6 %copy-start.34 = (f32[128]{0:T(128)}, f32[128]{0:T(128)S(1)}, u32[]{:S(2)}) copy-start(f32[128]{0:T(128)S(1)} %broadcast_multiply_fusion.1) | copy-start | bytes 1540
  22.5 56.9 %copy-start.36 = (f32[128]{0:T(128)}, f32[128]{0:T(128)S(1)}, u32[]{:S(2)}) copy-start(f32[128]{0:T(128)S(1)} %fusion.65) | copy-start | bytes 1540
  80.1 213.6 %all-gather.19.cloned.1.call-start = ((), (), s32[]{:S(2)}) async-start(), calls=%async_computation.7 | async-start | bytes 8650752 | tf_op jit(solution)/shard_map/all_gather | solution.py:198
  85.4 7.8 copy-start.33
  85.4 103.1 %copy-start.38 = (bf16[1024]{0:T(1024)(128)(2,1)S(1)}, bf16[1024]{0:T(1024)(128)(2,1)}, u32[]{:S(2)}) copy-start(bf16[1024]{0:T(1024)(128)(2,1)} %param.30) | copy-start | bytes 6148
  85.4 108.3 %copy-start.43 = (bf16[256]{0:T(256)(128)(2,1)S(1)}, bf16[256]{0:T(256)(128)(2,1)}, u32[]{:S(2)}) copy-start(bf16[256]{0:T(256)(128)(2,1)} %param.28) | copy-start | bytes 1540
  85.4 113.3 %copy-start.44 = (bf16[256]{0:T(256)(128)(2,1)S(1)}, bf16[256]{0:T(256)(128)(2,1)}, u32[]{:S(2)}) copy-start(bf16[256]{0:T(256)(128)(2,1)} %param.27) | copy-start | bytes 1540
  86.3 319.8 %all-gather.21.cloned.1.call-start = ((), (), s32[]{:S(2)}) async-start(), calls=%async_computation.8 | async-start | bytes 2621440 | tf_op jit(solution)/shard_map/all_gather | solution.py:159
  86.8 321.7 %all-gather.23.cloned.1.call-start = ((), (), s32[]{:S(2)}) async-start(), calls=%async_computation.9 | async-start | bytes 10485760 | tf_op jit(solution)/shard_map/all_gather | solution.py:165
  87.4 401.2 %all-gather.25.cloned.1.call-start = ((), (), s32[]{:S(2)}) async-start(), calls=%async_computation.10 | async-start | bytes 10485760 | tf_op jit(solution)/shard_map/all_gather | solution.py:167
  88.0 922.5 %reduce-scatter.6.cloned.1.call-start = ((), (), s32[]{:S(2)}) async-start(), calls=%async_computation.11 | async-start | bytes 17301504 | tf_op jit(solution)/shard_map/reduce_scatter | solution.py:271
  305.2 100.9 %copy-start.7 = (bf16[1,128,1024]{2,1,0:T(8,128)(2,1)S(1)}, bf16[1,128,1024]{2,1,0:T(8,128)(2,1)}, u32[]{:S(2)}) copy-start(bf16[1,128,1024]{2,1,0:T(8,128)(2,1)} %param.19) | copy-start | bytes 786436
  408.3 91.1 %copy-start.4 = (f32[128,1024]{1,0:T(8,128)}, f32[128,1024]{1,0:T(8,128)S(1)}, u32[]{:S(2)}) copy-start(f32[128,1024]{1,0:T(8,128)S(1)} %get-tuple-element.372) | copy-start | bytes 1572868
  408.6 80.0 %copy-start.15 = (bf16[1,128,1024]{2,1,0:T(8,128)(2,1)S(1)}, bf16[1,128,1024]{2,1,0:T(8,128)(2,1)}, u32[]{:S(2)}) copy-start(bf16[1,128,1024]{2,1,0:T(8,128)(2,1)} %param.33) | copy-start | bytes 786436
  413.4 82.9 %copy-start.9 = (f32[128,4096]{1,0:T(8,128)}, f32[128,4096]{1,0:T(8,128)S(1)}, u32[]{:S(2)}) copy-start(f32[128,4096]{1,0:T(8,128)S(1)} %convolution_add_fusion) | copy-start | bytes 6291460
  488.6 7.7 copy-start.3
  645.6 396.5 %reduce-scatter.10.cloned.1.call-start = ((), (), s32[]{:S(2)}) async-start(), calls=%async_computation.13 | async-start | bytes 2621440 | tf_op jit(solution)/shard_map/reduce_scatter | solution.py:294
  648.6 476.2 %reduce-scatter.12.cloned.1.call-start = ((), (), s32[]{:S(2)}) async-start(), calls=%async_computation.14 | async-start | bytes 10485760 | tf_op jit(solution)/shard_map/reduce_scatter | solution.py:312
  654.4 553.0 %reduce-scatter.14.cloned.1.call-start = ((), (), s32[]{:S(2)}) async-start(), calls=%async_computation.15 | async-start | bytes 10485760 | tf_op jit(solution)/shard_map/reduce_scatter | solution.py:318
  661.6 348.9 %copy-start.8 = (bf16[1,128,1024]{2,1,0:T(8,128)(2,1)S(1)}, bf16[1,128,1024]{2,1,0:T(8,128)(2,1)}, u32[]{:S(2)}) copy-start(bf16[1,128,1024]{2,1,0:T(8,128)(2,1)} %param.19) | copy-start | bytes 786436
  661.6 348.9 %copy-start.30 = (f32[4,1,256]{2,1,0:T(1,128)S(1)}, f32[4,1,256]{2,1,0:T(1,128)}, u32[]{:S(2)}) copy-start(f32[4,1,256]{2,1,0:T(1,128)} %copy-done.29) | copy-start | bytes 12292
  661.6 348.9 %copy-start.32 = (f32[4,1,256]{2,1,0:T(1,128)S(1)}, f32[4,1,256]{2,1,0:T(1,128)}, u32[]{:S(2)}) copy-start(f32[4,1,256]{2,1,0:T(1,128)} %copy-done.31) | copy-start | bytes 12292
  661.6 348.9 %copy-start.35 = (f32[128]{0:T(128)S(1)}, f32[128]{0:T(128)}, u32[]{:S(2)}) copy-start(f32[128]{0:T(128)} %copy-done.34) | copy-start | bytes 1540
  661.7 348.9 %copy-start.37 = (f32[128]{0:T(128)S(1)}, f32[128]{0:T(128)}, u32[]{:S(2)}) copy-start(f32[128]{0:T(128)} %copy-done.36) | copy-start | bytes 1540
  661.7 611.8 %reduce-scatter.8.cloned.1.call-start = ((), (), s32[]{:S(2)}) async-start(), calls=%async_computation.12 | async-start | bytes 7864320 | tf_op jit(solution)/shard_map/reduce_scatter | solution.py:288
  1016.2 641.3 %all-reduce.13.cloned.1.call-start = ((), (), s32[]{:S(2)}) async-start(), calls=%async_computation.16 | async-start | bytes 12582912 | tf_op jit(solution)/shard_map/psum | solution.py:326
  1273.5 5.8 copy-start.46
  1287.7 119.8 %copy-start.14 = (f32[128,1024]{1,0:T(8,128)S(1)}, f32[128,1024]{1,0:T(8,128)}, u32[]{:S(2)}) copy-start(f32[128,1024]{1,0:T(8,128)} %copy-done.13) | copy-start | bytes 1572868
  (55 other events, 172.8 us)
Sparse Core Ops, SparseCore 0:
  9.7 65.5 all-gather.14
  80.2 107.0 all-gather.16
  190.9 102.7 all-gather.18
  295.2 26.6 all-gather.20
  323.4 81.2 all-gather.22
  406.2 82.3 all-gather.24
  645.7 364.7 reduce-scatter.5
  1013.5 28.6 reduce-scatter.9
  1044.7 80.0 reduce-scatter.11
  1127.3 80.0 reduce-scatter.13
  1209.9 63.4 reduce-scatter.7
  1276.3 381.1 all-reduce.12
where the time goes:
time: 1680 us; the launch traced here: 1670 us
  waiting for transfers between devices  1060 us (63%)
  blocking collectives  244 us (15%)
  matrix products  183 us (11%)
  local copies, waits for them, and re-layouts  97.9 us (6%)
  other arithmetic  68.6 us (4%)
  between operations  17.2 us (1%)
    reduce_scatter x1, waiting for transfers between devices, body(): lax.psum_scatter(kv_terms.reshape(total_rows, 2 * width).astype(jnp.bfloa...  346 us
    psum x1, waiting for transfers between devices, body(): lax.psum(shares[0].astype(jnp.bfloat16), 'ctx').astype(jnp.float32)  249 us
    psum x1, blocking collectives, body(): lax.psum(shares[1].astype(jnp.bfloat16), 'ctx').astype(jnp.float32)  96.4 us
    all_gather x1, blocking collectives, body(): key_places = lax.all_gather(query_places, 'ctx', axis=0, tiled=True)  94.1 us
    reduce_scatter x1, waiting for transfers between devices, body(): lax.psum_scatter(grad_wup.astype(jnp.bfloat16), 'wsh', scatter_dimension=...  82.7 us
    reduce_scatter x1, waiting for transfers between devices, body(): lax.psum_scatter(grad_wdown.astype(jnp.bfloat16), 'wsh', scatter_dimensio...  82.6 us
    all_gather x1, waiting for transfers between devices, body(): lax.all_gather(values, 'ctx', axis=0, tiled=True)  78.2 us
    all_gather x1, waiting for transfers between devices, body(): lax.all_gather(w_down, 'wsh', axis=0, tiled=True)  75.2 us
  transfers between devices with their start and end apart: 12, of which 9 were waited for; matrix products, arithmetic and copies ran while one was open for 10% of the time, Pallas kernels for 0%

commit v1 on v0

v1 whole, which is shorter than its diff:
```python
import functools

import jax
import jax.numpy as jnp
from jax import lax
from jax.experimental import pallas as pl
from jax.experimental.pallas import tpu as pltpu
from jax.sharding import PartitionSpec as P

HEADS = 16
HEAD_DIM = 64
EPS = 1e-05
NEGATIVE = -1e30
RUN = 64
Q_TILE = 256
K_TILE = 512
F32 = jnp.float32
BF16 = jnp.bfloat16
VMEM = pl.BlockSpec(memory_space=pltpu.VMEM)
SMEM = pl.BlockSpec(memory_space=pltpu.SMEM)
PARAMS = pltpu.CompilerParams(vmem_limit_bytes=48 * 1024 * 1024)


def layer_norm(values, gain_vec, shift_vec):
    average = jnp.mean(values, axis=-1, keepdims=True)
    centred = values - average
    variance = jnp.mean(centred * centred, axis=-1, keepdims=True)
    return centred * lax.rsqrt(variance + EPS) * gain_vec + shift_vec


def gelu_tanh(values):
    return (
        0.5
        * values
        * (1.0 + jnp.tanh(0.7978845608028654 * (values + 0.044715 * values * values * values)))
    )


def dot(left, right, left_dim, right_dim):
    return lax.dot_general(
        left, right, (((left_dim,), (right_dim,)), ((), ())), preferred_element_type=F32
    )


def pack_qkv_kernel(mixed_ref, bias_ref, out_ref):
    for slot in range(4):
        for head in range(4):
            parts = [[], []]
            for half in range(2):
                rows = pl.ds(slot * 128 + half * RUN, RUN)
                for part in range(3):
                    cols = pl.ds(part * 256 + head * HEAD_DIM, HEAD_DIM)
                    parts[half].append(mixed_ref[rows, cols] + bias_ref[:, cols])
            (qe, ke, ve), (ql, kl, vl) = parts
            out_ref[slot * 4 + head] = jnp.concatenate([qe, ql, ke, ve, kl, vl], axis=1).astype(
                BF16
            )


def pack_qkv(mixed, bias):
    return pl.pallas_call(
        pack_qkv_kernel,
        out_shape=jax.ShapeDtypeStruct((16, RUN, 384), BF16),
        in_specs=[VMEM, VMEM],
        out_specs=VMEM,
        compiler_params=PARAMS,
    )(mixed, bias)


def pack_heads_kernel(flat_ref, out_ref):
    for slot in range(4):
        for head in range(4):
            cols = pl.ds(head * HEAD_DIM, HEAD_DIM)
            out_ref[slot * 4 + head] = jnp.concatenate(
                [
                    flat_ref[pl.ds(slot * 128, RUN), cols],
                    flat_ref[pl.ds(slot * 128 + RUN, RUN), cols],
                ],
                axis=1,
            ).astype(BF16)


def pack_heads(flat):
    return pl.pallas_call(
        pack_heads_kernel,
        out_shape=jax.ShapeDtypeStruct((16, RUN, 128), BF16),
        in_specs=[VMEM],
        out_specs=VMEM,
        compiler_params=PARAMS,
    )(flat)


def unpack_heads_kernel(packed_ref, out_ref):
    for slot in range(4):
        for half in range(2):
            rows = pl.ds(slot * 128 + half * RUN, RUN)
            out_ref[rows, :] = jnp.concatenate(
                [
                    packed_ref[slot * 4 + head, :, pl.ds(half * HEAD_DIM, HEAD_DIM)]
                    for head in range(4)
                ],
                axis=1,
            )


def unpack_heads(packed):
    return pl.pallas_call(
        unpack_heads_kernel,
        out_shape=jax.ShapeDtypeStruct((512, 256), BF16),
        in_specs=[VMEM],
        out_specs=VMEM,
        compiler_params=PARAMS,
    )(packed)


def unpack_qkv_kernel(packed_ref, out_ref):
    starts = ((0, 128, 192), (64, 256, 320))
    for slot in range(4):
        for half in range(2):
            rows = pl.ds(slot * 128 + half * RUN, RUN)
            out_ref[rows, :] = jnp.concatenate(
                [
                    packed_ref[slot * 4 + head, :, pl.ds(starts[half][part], HEAD_DIM)]
                    for part in range(3)
                    for head in range(4)
                ],
                axis=1,
            )


def unpack_qkv(packed):
    return pl.pallas_call(
        unpack_qkv_kernel,
        out_shape=jax.ShapeDtypeStruct((512, 768), BF16),
        in_specs=[VMEM],
        out_specs=VMEM,
        compiler_params=PARAMS,
    )(packed)


def run_rows(index):
    return pl.ds(pl.multiple_of(index * RUN, RUN), RUN)


def query_places(sorted_ref, tile):
    lane = lax.broadcasted_iota(jnp.int32, (1, Q_TILE), 1)
    base = jnp.zeros((1, Q_TILE), jnp.int32)
    for block in range(Q_TILE // RUN):
        start = sorted_ref[tile * (Q_TILE // RUN) + block] * RUN - block * RUN
        base = jnp.where(lane // RUN == block, start, base)
    return base + lane


def chunk_bounds(sorted_ref, tile):
    per = Q_TILE // RUN
    lowest = sorted_ref[tile * per] * RUN
    highest = sorted_ref[tile * per + per - 1] * RUN + RUN
    return lowest // K_TILE, (highest + K_TILE - 1) // K_TILE


def sort_queries(scalar_ref, sorted_ref):
    for index in range(32):
        sorted_ref[scalar_ref[index]] = scalar_ref[32 + index]


def attend_kernel(
    scalar_ref, slope_ref, own_ref, other_ref,
    out_ref, q_ref, k_ref, v_ref, exact_ref, log_ref,
    sorted_ref, vt_ref, rows_ref,
):
    sort_queries(scalar_ref, sorted_ref)
    for source in range(16):
        for half in range(2):
            index = source * 2 + half
            cols = half * HEAD_DIM
            q_ref[run_rows(scalar_ref[index]), :] = (
                own_ref[source, :, pl.ds(cols, HEAD_DIM)].astype(F32) * HEAD_DIM ** (-0.5)
            ).astype(BF16)
            place = run_rows(scalar_ref[32 + index])
            k_ref[place, :] = own_ref[source, :, pl.ds(128 + half * 128, HEAD_DIM)]
            v_ref[place, :] = own_ref[source, :, pl.ds(192 + half * 128, HEAD_DIM)]
            place = run_rows(scalar_ref[64 + index])
            k_ref[place, :] = other_ref[source, :, pl.ds(half * 128, HEAD_DIM)]
            v_ref[place, :] = other_ref[source, :, pl.ds(64 + half * 128, HEAD_DIM)]
    for chunk in range(4096 // K_TILE):
        rows = pl.ds(chunk * K_TILE, K_TILE)
        vt_ref[:, rows] = v_ref[rows, :].T
    slope = slope_ref[0]
    ramp = lax.broadcasted_iota(jnp.int32, (K_TILE, Q_TILE), 0)
    bias = ramp.astype(F32) * slope

    def tile_step(tile, unused):
        q_rows = pl.ds(pl.multiple_of(tile * Q_TILE, Q_TILE), Q_TILE)
        query = q_ref[q_rows, :]
        places = query_places(sorted_ref, tile)
        full, every = chunk_bounds(sorted_ref, tile)

        def chunk_step(masked, chunk, carry):
            highest, total, accum = carry
            k_rows = pl.ds(pl.multiple_of(chunk * K_TILE, K_TILE), K_TILE)
            scores = dot(k_ref[k_rows, :], query, 1, 1) + bias
            if masked:
                scores = jnp.where(ramp <= places - chunk * K_TILE, scores, NEGATIVE)
            offset = slope * (chunk * K_TILE).astype(F32)
            new_high = jnp.maximum(highest, jnp.max(scores, axis=0, keepdims=True) + offset)
            weights = jnp.exp(scores - (new_high - offset))
            factor = jnp.exp(highest - new_high)
            total = total * factor + jnp.sum(weights, axis=0, keepdims=True)
            accum = accum * factor + dot(vt_ref[:, k_rows], weights.astype(BF16), 1, 0)
            return new_high, total, accum

        carry = (
            jnp.full((1, Q_TILE), NEGATIVE, F32),
            jnp.zeros((1, Q_TILE), F32),
            jnp.zeros((HEAD_DIM, Q_TILE), F32),
        )
        carry = lax.fori_loop(0, full, functools.partial(chunk_step, False), carry)
        highest, total, accum = lax.fori_loop(
            full, every, functools.partial(chunk_step, True), carry
        )
        exact = accum / total
        exact_ref[:, q_rows] = exact
        log_ref[:, q_rows] = highest + jnp.log(total)
        rows_ref[q_rows, :] = exact.T
        return unused

    lax.fori_loop(0, 2048 // Q_TILE, tile_step, 0)
    for source in range(16):
        out_ref[source] = jnp.concatenate(
            [rows_ref[run_rows(scalar_ref[source * 2 + half]), :] for half in range(2)], axis=1
        ).astype(BF16)


def attend(scalars, slope, own, other):
    return pl.pallas_call(
        attend_kernel,
        out_shape=(
            jax.ShapeDtypeStruct((16, RUN, 128), BF16),
            jax.ShapeDtypeStruct((2048, HEAD_DIM), BF16),
            jax.ShapeDtypeStruct((4096, HEAD_DIM), BF16),
            jax.ShapeDtypeStruct((4096, HEAD_DIM), BF16),
            jax.ShapeDtypeStruct((HEAD_DIM, 2048), F32),
            jax.ShapeDtypeStruct((1, 2048), F32),
        ),
        in_specs=[SMEM, SMEM, VMEM, VMEM],
        out_specs=(VMEM,) * 6,
        scratch_shapes=[
            pltpu.SMEM((32,), jnp.int32),
            pltpu.VMEM((HEAD_DIM, 4096), BF16),
            pltpu.VMEM((2048, HEAD_DIM), F32),
        ],
        compiler_params=PARAMS,
    )(scalars, slope, own, other)


def attend_back_kernel(
    scalar_ref, slope_ref, grad_ref, q_ref, k_ref, v_ref, exact_ref, log_ref,
    dq_out, own_out, other_out,
    sorted_ref, kt_ref, do_ref, dq_ref, dk_ref, dv_ref,
):
    sort_queries(scalar_ref, sorted_ref)
    for source in range(16):
        for half in range(2):
            do_ref[run_rows(scalar_ref[source * 2 + half]), :] = grad_ref[
                source, :, pl.ds(half * HEAD_DIM, HEAD_DIM)
            ]
    for chunk in range(4096 // K_TILE):
        rows = pl.ds(chunk * K_TILE, K_TILE)
        kt_ref[:, rows] = k_ref[rows, :].T
    dk_ref[...] = jnp.zeros_like(dk_ref)
    dv_ref[...] = jnp.zeros_like(dv_ref)
    slope = slope_ref[0]
    ramp = lax.broadcasted_iota(jnp.int32, (K_TILE, Q_TILE), 0)
    bias = ramp.astype(F32) * slope

    def tile_step(tile, unused):
        q_rows = pl.ds(pl.multiple_of(tile * Q_TILE, Q_TILE), Q_TILE)
        query = q_ref[q_rows, :]
        d_out = do_ref[q_rows, :]
        places = query_places(sorted_ref, tile)
        full, every = chunk_bounds(sorted_ref, tile)
        log_rows = log_ref[:, q_rows]
        delta = jnp.sum(d_out.astype(F32).T * exact_ref[:, q_rows], axis=0, keepdims=True)

        def chunk_step(masked, chunk, dq):
            k_rows = pl.ds(pl.multiple_of(chunk * K_TILE, K_TILE), K_TILE)
            scores = dot(k_ref[k_rows, :], query, 1, 1) + bias
            offset = slope * (chunk * K_TILE).astype(F32)
            if masked:
                scores = jnp.where(ramp <= places - chunk * K_TILE, scores, NEGATIVE)
            weights = jnp.exp(scores - (log_rows - offset))
            d_weights = dot(v_ref[k_rows, :], d_out, 1, 1)
            d_scores = (weights * (d_weights - delta)).astype(BF16)
            dv_ref[k_rows, :] += dot(weights.astype(BF16), d_out, 1, 0)
            dk_ref[k_rows, :] += dot(d_scores, query, 1, 0)
            return dq + dot(kt_ref[:, k_rows], d_scores, 1, 0)

        dq = jnp.zeros((HEAD_DIM, Q_TILE), F32)
        dq = lax.fori_loop(0, full, functools.partial(chunk_step, False), dq)
        dq = lax.fori_loop(full, every, functools.partial(chunk_step, True), dq)
        dq_ref[q_rows, :] = (dq * HEAD_DIM ** (-0.5)).T
        return unused

    lax.fori_loop(0, 2048 // Q_TILE, tile_step, 0)
    for source in range(16):
        dq_out[source] = jnp.concatenate(
            [dq_ref[run_rows(scalar_ref[source * 2 + half]), :] for half in range(2)], axis=1
        ).astype(BF16)
        for base, target in ((32, own_out), (64, other_out)):
            parts = []
            for half in range(2):
                place = run_rows(scalar_ref[base + source * 2 + half])
                parts += [dk_ref[place, :], dv_ref[place, :]]
            target[source] = jnp.concatenate(parts, axis=1).astype(target.dtype)


def attend_back(scalars, slope, grad, q, k, v, exact, logs):
    return pl.pallas_call(
        attend_back_kernel,
        out_shape=(
            jax.ShapeDtypeStruct((16, RUN, 128), BF16),
            jax.ShapeDtypeStruct((16, RUN, 256), F32),
            jax.ShapeDtypeStruct((16, RUN, 256), BF16),
        ),
        in_specs=[SMEM, SMEM] + [VMEM] * 6,
        out_specs=(VMEM,) * 3,
        scratch_shapes=[
            pltpu.SMEM((32,), jnp.int32),
            pltpu.VMEM((HEAD_DIM, 4096), BF16),
            pltpu.VMEM((2048, HEAD_DIM), BF16),
            pltpu.VMEM((2048, HEAD_DIM), F32),
            pltpu.VMEM((4096, HEAD_DIM), F32),
            pltpu.VMEM((4096, HEAD_DIM), F32),
        ],
        compiler_params=PARAMS,
    )(scalars, slope, grad, q, k, v, exact, logs)


PLANES = [[2 * i + z for i in range(16)] for z in range(2)]


def swap(value, slot):
    return lax.ppermute(value, "wsh", [(i, i ^ slot) for i in range(4)])


def gather_slots(value):
    return jnp.stack([value] + [swap(value, slot) for slot in (1, 2, 3)])


def reduce_slots(partial):
    rows = partial.reshape(4, 128, -1)
    total = rows[0]
    for slot in (1, 2, 3):
        total = total + swap(rows[slot].astype(BF16), slot).astype(F32)
    return total


def in_order(slots, rank):
    return [
        lax.dynamic_index_in_dim(slots, jnp.bitwise_xor(rank, i), 0, keepdims=False)
        for i in range(4)
    ]


def head_exchange(value):
    return lax.all_to_all(value, "ctx", 0, 0, axis_index_groups=PLANES, tiled=True)


def partner(value):
    return lax.ppermute(value, "ctx", [(i, i ^ 1) for i in range(32)])


def sum_pieces(pieces):
    received = lax.all_to_all(pieces, "ctx", 0, 0, tiled=True)
    return jnp.sum(received.astype(F32), axis=0)


def body(
    tokens,
    places,
    w_qkv,
    b_qv,
    w_out,
    b_out,
    norm1_gain,
    norm1_shift,
    norm2_gain,
    norm2_shift,
    w_up,
    b_up,
    w_down,
    b_down,
    cotangent,
):
    rank = lax.axis_index("wsh")
    column = lax.axis_index("ctx")
    plane = column % 2
    head = rank * 4 + (column // 2) % 4

    runs = places[0].reshape(2, RUN)[:, 0] // RUN
    small = jnp.concatenate(
        [
            b_qv, b_out, norm1_gain, norm1_shift, norm2_gain, norm2_shift, b_up, b_down,
            runs.astype(BF16), jnp.zeros((126,), BF16),
        ]
    )
    small = lax.all_gather(small, "wsh", axis=0).astype(F32)
    full_bqv = small[:, 0:512].reshape(-1)
    full_bout = small[:, 512:768].reshape(-1)
    gain_one = small[:, 768:1024].reshape(-1)
    shift_one = small[:, 1024:1280].reshape(-1)
    gain_two = small[:, 1280:1536].reshape(-1)
    shift_two = small[:, 1536:1792].reshape(-1)
    bias_up = lax.dynamic_index_in_dim(small[:, 1792:2816], rank, 0)
    full_bdown = small[:, 2816:3072].reshape(-1)
    slot_runs = jnp.stack(in_order(small[:, 3072:3074], rank))
    runs_out = jnp.broadcast_to(slot_runs[:, None, None, :], (4, 4, 2, 2)).reshape(32, 1, 2)
    runs_out = jnp.pad(jnp.broadcast_to(runs_out, (32, 8, 2)), ((0, 0), (0, 0), (0, 126)))
    all_runs = lax.all_to_all(runs_out, "ctx", 0, 0, tiled=True)[:, 0, :2].astype(jnp.int32)
    all_runs = all_runs.reshape(16, 2, 2)
    own_runs = lax.dynamic_index_in_dim(all_runs, plane, 1, keepdims=False).reshape(32)
    other_runs = lax.dynamic_index_in_dim(all_runs, 1 - plane, 1, keepdims=False).reshape(32)
    ranks = jnp.sum((own_runs[None, :] < own_runs[:, None]).astype(jnp.int32), axis=1)
    scalars = jnp.concatenate([ranks, own_runs, other_runs])
    slope = (
        8.0 * jnp.exp2(-4.0 * (head.astype(F32) + 1.0) / HEADS) / 4096.0
    ).reshape(1)

    token_slots = gather_slots(tokens[0])
    qkv_cols = w_qkv.reshape(256, 3, 4, 256)
    pieces = []
    for slot in range(4):
        piece = lax.dynamic_index_in_dim(
            qkv_cols, jnp.bitwise_xor(rank, slot), 2, keepdims=False
        ).reshape(256, 768)
        pieces.append(swap(piece, slot) if slot else piece)
    part_qkv = jnp.concatenate(in_order(jnp.stack(pieces), rank), axis=0)
    pieces = []
    for slot in range(4):
        piece = lax.dynamic_slice_in_dim(w_up, jnp.bitwise_xor(rank, slot) * 1024, 1024, 1)
        pieces.append(swap(piece, slot) if slot else piece)
    part_up = jnp.concatenate(in_order(jnp.stack(pieces), rank), axis=0)
    d_down = gather_slots(cotangent[0]).reshape(512, 1024)

    normed_one = layer_norm(token_slots.astype(F32), gain_one, shift_one)
    normed_one = normed_one.astype(BF16).reshape(512, 1024)
    mixed = dot(normed_one, part_qkv, 1, 0)
    bias_qkv = jnp.concatenate(
        [
            lax.dynamic_slice_in_dim(full_bqv, rank * 256, 256),
            jnp.zeros((256,), F32),
            lax.dynamic_slice_in_dim(full_bqv, 1024 + rank * 256, 256),
        ]
    ).reshape(1, 768)
    own = head_exchange(pack_qkv(mixed, bias_qkv))
    other = partner(own[:, :, 128:])
    out_packed, q, k, v, exact, logs = attend(scalars, slope, own, other)
    attended = unpack_heads(head_exchange(out_packed))

    residual_in = tokens[0].astype(F32)
    middle = residual_in + reduce_slots(dot(attended, w_out, 1, 0)) + full_bout
    normed_two, norm_two_back = jax.vjp(layer_norm, middle, gain_two, shift_two)
    normed_two = gather_slots(normed_two.astype(BF16)).reshape(512, 1024)
    pre_act = dot(normed_two, part_up, 1, 0) + bias_up
    hidden, gelu_back = jax.vjp(gelu_tanh, pre_act)
    hidden = hidden.astype(BF16)
    output = middle + reduce_slots(dot(hidden, w_down, 1, 0)) + full_bdown

    (d_pre,) = gelu_back(dot(d_down, w_down, 1, 1))
    d_pre = d_pre.astype(BF16)
    d_normed_two = reduce_slots(dot(d_pre, part_up, 1, 1))
    d_norm_two, grad_gain_two, grad_shift_two = norm_two_back(d_normed_two)
    d_output = cotangent[0].astype(F32)
    d_middle = d_output + d_norm_two
    d_branch_own = d_middle.astype(BF16)
    d_branch = gather_slots(d_branch_own).reshape(512, 1024)
    d_attended = dot(d_branch, w_out, 1, 1)

    grad = head_exchange(pack_heads(d_attended))
    dq, dkv_own, dkv_other = attend_back(scalars, slope, grad, q, k, v, exact, logs)
    dkv = (dkv_own + partner(dkv_other).astype(F32)).astype(BF16)
    d_mixed = unpack_qkv(head_exchange(jnp.concatenate([dq, dkv], axis=2)))
    d_normed_one = reduce_slots(dot(d_mixed, part_qkv, 1, 1))
    _, norm_one_back = jax.vjp(layer_norm, residual_in, gain_one, shift_one)
    d_norm_one, grad_gain_one, grad_shift_one = norm_one_back(d_normed_one)
    grad_input = d_middle + d_norm_one

    def row_pieces(grad):
        slots = jnp.stack(in_order(grad.astype(BF16).reshape(4, 32, 8, -1), rank), axis=1)
        return slots.reshape(32, 32, -1)

    def to_owners(pieces, parts):
        slots = pieces.astype(BF16).reshape(4, 8, -1)
        slots = jnp.stack([slots[0]] + [swap(slots[s], s) for s in (1, 2, 3)])
        columns = jnp.stack(in_order(slots, rank)).reshape(4, 8, parts, -1)
        return columns.transpose(2, 1, 0, 3).reshape(parts * 8, -1)

    grad_wdown = dot(hidden, d_down, 0, 0)
    grad_wup = dot(normed_two, d_pre, 0, 0)
    grad_wout = dot(attended, d_branch, 0, 0)
    early = jnp.concatenate(
        [
            grad_wdown.astype(BF16).reshape(32, 32, 1024),
            row_pieces(grad_wup),
            grad_wout.astype(BF16).reshape(32, 8, 1024),
        ],
        axis=1,
    )
    early = sum_pieces(early)
    up_rows = to_owners(early[32:64], 1).reshape(8, 4, 1024).transpose(1, 0, 2).reshape(32, 1024)
    early = jnp.concatenate([early[:32].astype(BF16), up_rows, early[64:].astype(BF16)], axis=0)
    early = lax.all_gather(early, "ctx", axis=0)

    grad_wqkv = dot(normed_one, d_mixed, 0, 0)
    sums = jnp.sum(d_mixed.astype(F32), axis=0)
    grad_bqv = jnp.zeros((2048,), F32)
    grad_bqv = lax.dynamic_update_slice_in_dim(grad_bqv, sums[:256], rank * 256, 0)
    grad_bqv = lax.dynamic_update_slice_in_dim(grad_bqv, sums[512:], 1024 + rank * 256, 0)
    grad_bup = lax.dynamic_update_slice_in_dim(
        jnp.zeros((4, 1024), F32), jnp.sum(d_pre.astype(F32), axis=0)[None], rank, 0
    )
    vectors = jnp.concatenate(
        [
            grad_bqv.reshape(4, 512),
            jnp.sum(d_branch_own.astype(F32), axis=0).reshape(4, 256),
            grad_gain_one.reshape(4, 256),
            grad_shift_one.reshape(4, 256),
            grad_gain_two.reshape(4, 256),
            grad_shift_two.reshape(4, 256),
            grad_bup,
            jnp.sum(d_output, axis=0).reshape(4, 256),
        ],
        axis=1,
    )
    vectors = jnp.stack(in_order(vectors, rank)).reshape(4, 32, 96).transpose(1, 0, 2)
    vectors = jnp.pad(vectors, ((0, 0), (0, 4), (0, 672)))
    late = jnp.concatenate([row_pieces(grad_wqkv), vectors.astype(BF16)], axis=1)
    late = sum_pieces(late)
    mine = late[32:36, :128].astype(BF16)
    vector = mine[0].astype(F32)
    for slot in (1, 2, 3):
        vector = vector + swap(mine[slot], slot).astype(F32)
    vector = jnp.pad(vector.astype(BF16).reshape(1, 128), ((0, 7), (0, 896)))
    late = jnp.concatenate([to_owners(late[:32], 3).reshape(24, 1024), vector], axis=0)
    late = lax.all_gather(late, "ctx", axis=0)

    out_wdown = early[:, :32].astype(F32).reshape(1024, 1024)
    out_wup = early[:, 32:64].astype(F32).reshape(32, 4, 8, 1024)
    out_wup = out_wup.transpose(0, 2, 1, 3).reshape(256, 4096)
    out_wout = early[:, 64:].astype(F32).reshape(256, 1024)
    out_wqkv = late[:, :24].astype(F32).reshape(32, 3, 8, 1024)
    out_wqkv = out_wqkv.transpose(0, 2, 1, 3).reshape(256, 3072)
    out_vec = late[:, 24, :96].astype(F32).reshape(3072)
    return (
        output.astype(BF16)[None],
        grad_input.astype(BF16)[None],
        out_wqkv,
        out_vec[0:512],
        out_wout,
        out_vec[512:768],
        out_vec[768:1024],
        out_vec[1024:1280],
        out_vec[1280:1536],
        out_vec[1536:1792],
        out_wup,
        out_vec[1792:2816],
        out_wdown,
        out_vec[2816:3072],
    )


def solution(mesh):
    rows = P("wsh", "ctx", None)
    matrix = P("wsh", None)
    vector = P("wsh")
    return jax.shard_map(
        body,
        mesh=mesh,
        in_specs=(
            rows, P("wsh", "ctx"), matrix, vector, matrix, vector, vector, vector, vector, vector,
            matrix, vector, matrix, vector, rows,
        ),
        out_specs=(
            rows, rows, matrix, vector, matrix, vector, vector, vector, vector, vector,
            matrix, vector, matrix, vector,
        ),
        check_vma=False,
    )
```

time: 1680 us -> 600 us (0.36)
  waiting for transfers between devices: 1060 us -> 338 us
  blocking collectives: 244 us -> 31 us
  matrix products: 183 us -> 20.6 us
  starting transfers between devices: 0.73 us -> 66.8 us
  local copies, waits for them, and re-layouts: 97.9 us -> 34.8 us
  Pallas kernels: 0 us -> 45.2 us
  other arithmetic: 68.6 us -> 38.7 us
    reduce_scatter x5 -> x0, waiting for transfers between devices: 603 us -> none  [the longest x1 346 us: body(): lax.psum_scatter(kv_terms.reshape(total_rows, 2 * width).astype(jnp.bfloa...]
    psum x1 -> x0, waiting for transfers between devices: 249 us -> none  [body(): lax.psum(shares[0].astype(jnp.bfloat16), 'ctx').astype(jnp.float32)]
    dot_general x68 -> x12, matrix products: 183 us -> 20.6 us  [dot(): lax.dot_general(left, right, (((left_dim,), (right_dim,)), ((), ())), pre...]
    all_gather x9 -> x1, blocking collectives: 135 us -> 15.2 us  [body(): small = lax.all_gather(small, 'wsh', axis=0).astype(F32)]
    all_to_all x0 -> x6, waiting for transfers between devices: none -> 111 us  [the longest x2 71.6 us: sum_pieces(): received = lax.all_to_all(pieces, 'ctx', 0, 0, tiled=True)]
    ppermute x0 -> x41, waiting for transfers between devices: none -> 106 us  [the longest x39 94.2 us: swap(): return lax.ppermute(value, 'wsh', [(i, i ^ slot) for i in range(4)])]
    psum x1 -> x0, blocking collectives: 96.4 us -> none  [body(): lax.psum(shares[1].astype(jnp.bfloat16), 'ctx').astype(jnp.float32)]
    all_gather x6 -> x2, waiting for transfers between devices: 206 us -> 122 us  [the longest x1 79.3 us: body(): early = lax.all_gather(early, 'ctx', axis=0)]
  transfers between devices with their start and end apart: 12 -> 49, of which waited for: 9 -> 29; matrix products, arithmetic and copies ran while one was open for 10% -> 9% of each run, Pallas kernels for 0% -> 4%
where the time goes in v1:
time: 600 us; the launch traced here: 591 us
  waiting for transfers between devices  338 us (56%)
  starting transfers between devices  66.8 us (11%)
  Pallas kernels  45.2 us (8%)
  other arithmetic  38.7 us (6%)
  local copies, waits for them, and re-layouts  34.8 us (6%)
  blocking collectives  31 us (5%)
  matrix products  20.6 us (3%)
  between operations  15.6 us (3%)
    ppermute x39, waiting for transfers between devices, swap(): return lax.ppermute(value, 'wsh', [(i, i ^ slot) for i in range(4)])  94.2 us
    all_gather x1, waiting for transfers between devices, body(): early = lax.all_gather(early, 'ctx', axis=0)  79.3 us
    all_to_all x2, waiting for transfers between devices, sum_pieces(): received = lax.all_to_all(pieces, 'ctx', 0, 0, tiled=True)  71.6 us
    all_gather x1, waiting for transfers between devices, body(): late = lax.all_gather(late, 'ctx', axis=0)  42.8 us
    all_to_all x3, waiting for transfers between devices, head_exchange(): lax.all_to_all(value, 'ctx', 0, 0, axis_index_groups=PLANES, tiled=True)  29.3 us
    ppermute x39, starting transfers between devices, swap(): return lax.ppermute(value, 'wsh', [(i, i ^ slot) for i in range(4)])  26.9 us
    pallas_call x1, Pallas kernels, attend(): pl.pallas_call(attend_kernel, out_shape=(jax.ShapeDtypeStruct((16, RUN, 1...  22.5 us
    pallas_call x1, Pallas kernels, attend_back(): pl.pallas_call(attend_back_kernel, out_shape=(jax.ShapeDtypeStruct((16, R...  21.8 us
  transfers between devices with their start and end apart: 49, of which 29 were waited for; matrix products, arithmetic and copies ran while one was open for 9% of the time, Pallas kernels for 4%

profile of v1, /device:TPU:0, one launch (start us, length us, event | category | flops | bytes accessed | tf_op | source)
XLA Modules:
  0.0 591.2 jit_solution(4554850486285206081)
XLA Ops:
  19.0 5.4 concatenate.33
  24.5 15.2 %all-gather.3 = bf16[4,1,3200]{2,1,0:T(2,128)(2,1)S(1)} all-gather(bf16[1,1,3200]{2,1,0:T(2,128)(2,1)S(1)} %reshape.392), channel_id=2, replica_groups=mesh['ctx'=32,'wsh'=4] {'wsh'}, dimensions={0}, use_global_device_ids=true | all-gather | bytes 32000 | tf_op jit(solution)/shard_map/all_gather | solution.py:407
  48.7 7.1 %all-to-all-start.1 = ((bf16[16,64,384]{2,1,0:T(8,128)(2,1)}), bf16[16,64,384]{2,1,0:T(8,128)(2,1)S(1)}, u32[]{:S(2)}, u32[]{:S(2)}) async-start(bf16[16,64,384]{2,1,0:T(8,128)(2,1)} %copy-done.2), calls=%async_computation.1 | async-start | bytes 1572864 | tf_op jit(solution)/shard_map/all_to_all | solution.py:366
  56.5 14.4 %all-to-all-done.1.own_ref = bf16[16,64,384]{2,1,0:T(8,128)(2,1)S(1)} async-done(((bf16[16,64,384]{2,1,0:T(8,128)(2,1)}), bf16[16,64,384]{2,1,0:T(8,128)(2,1)S(1)}, u32[]{:S(2)}, u32[]{:S(2)}) %all-to-all-start.1) | async-done | bytes 786464 | tf_op jit(solution)/shard_map/all_to_all | solution.py:366
  71.7 3.9 collective-permute-start.6
  80.4 9.8 %all-to-all-done = f32[32,8,128]{2,1,0:T(8,128)S(1)} async-done(((f32[32,8,128]{2,1,0:T(8,128)}), f32[32,8,128]{2,1,0:T(8,128)S(1)}, u32[]{:S(2)}, u32[]{:S(2)}) %all-to-all-start) | async-done | bytes 131104 | tf_op jit(solution)/shard_map/all_to_all | solution.py:419
  92.6 22.5 %shard_map.255 = (bf16[16,64,128]{2,1,0:T(8,128)(2,1)S(1)}, bf16[2048,64]{1,0:T(8,128)(2,1)S(1)}, bf16[4096,64]{1,0:T(8,128)(2,1)S(1)}, bf16[4096,64]{1,0:T(8,12...) custom-call(s32[96]{0:T(128)S(1)} %pad_add_fusion.scalar_ref, f32[1]{0:T(128)} %bitcast.2.slope_ref, ...), custom_call_target="tpu_custom_call" | custom-call | tf_op jit(solution)/shard_map/pallas_call | solution.py:235
  119.4 4.2 all-to-all-start.2
  136.3 5.1 collective-permute-done.15
  143.4 10.2 %collective-permute-done.14 = bf16[256,1024]{1,0:T(8,128)(2,1)} collective-permute-done((bf16[256,1024]{1,0:T(8,128)(2,1)}, bf16[256,1024]{1,0:T(8,128)(2,1)}, u32[]{:S(2)}, u32[]{:S(2)}) %collective-permute-start.14) | collective-permute-done | bytes 524320 | tf_op jit(solution)/shard_map/ppermute | solution.py:343
  158.1 6.0 %collective-permute-done.8 = bf16[128,1024]{1,0:T(8,128)(2,1)S(1)} collective-permute-done((bf16[128,1024]{1,0:T(8,128)(2,1)S(1)}, bf16[128,1024]{1,0:T(8,128)(2,1)S(1)}, u32[]{:S(2)}, u32[]{:S(2)}) %collective-permute-start.8) | collective-permute-done | bytes 262176 | tf_op jit(solution)/shard_map/ppermute | solution.py:343
  167.1 6.4 %collective-permute-done.12 = bf16[128,1024]{1,0:T(8,128)(2,1)S(1)} collective-permute-done((bf16[128,1024]{1,0:T(8,128)(2,1)S(1)}, bf16[128,1024]{1,0:T(8,128)(2,1)S(1)}, u32[]{:S(2)}, u32[]{:S(2)}) %collective-permute-start.12) | collective-permute-done | bytes 262176 | tf_op jit(solution)/shard_map/ppermute | solution.py:343
  173.5 5.6 collective-permute-done.11
  193.6 5.8 collective-permute-done.23
  199.8 4.6 collective-permute-done.18
  204.4 5.9 %collective-permute-done.17 = bf16[128,1024]{1,0:T(8,128)(2,1)S(1)} collective-permute-done((bf16[128,1024]{1,0:T(8,128)(2,1)S(1)}, bf16[128,1024]{1,0:T(8,128)(2,1)S(1)}, u32[]{:S(2)}, u32[]{:S(2)}) %collective-permute-start.17) | collective-permute-done | bytes 262176 | tf_op jit(solution)/shard_map/ppermute | solution.py:343
  213.7 6.6 %collective-permute-done.27 = bf16[128,1024]{1,0:T(8,128)(2,1)S(1)} collective-permute-done((bf16[128,1024]{1,0:T(8,128)(2,1)S(1)}, bf16[128,1024]{1,0:T(8,128)(2,1)S(1)}, u32[]{:S(2)}, u32[]{:S(2)}) %collective-permute-start.27) | collective-permute-done | bytes 262176 | tf_op jit(solution)/shard_map/ppermute | solution.py:343
  220.2 5.6 collective-permute-done.26
  227.6 15.7 %all_to_all.35.grad_ref = bf16[16,64,128]{2,1,0:T(8,128)(2,1)S(1)} all-to-all(bf16[16,64,128]{2,1,0:T(8,128)(2,1)S(1)} %shard_map.257), channel_id=1, replica_groups={{0,8,16,24,32,40,48,56,64,72,80,88,96,104,112,120},{4,12,20,28,36,44,52..., dimensions={0} | all-to-all | bytes 524288 | tf_op jit(solution)/shard_map/all_to_all | solution.py:366
  243.4 21.8 %shard_map.258 = (bf16[16,64,128]{2,1,0:T(8,128)(2,1)S(1)}, f32[16,64,256]{2,1,0:T(8,128)S(1)}, bf16[16,64,256]{2,1,0:T(8,128)(2,1)S(1)}) custom-call(s32[96]{0:T(128)S(1)} %pad_add_fusion.scalar_ref, f32[1]{0:T(128)} %bitcast.2.slope_ref, bf16[16,64,128]{2,1,0:T(8,128)(2,1)S(1)} %all_to_all.35.grad_ref, bf16[2048,64]{1,0:T(8,128)(2,1)S(1)} %copy-done.8, ...), custom_call_target="tpu_custom_call" | custom-call | tf_op jit(solution)/shard_map/pallas_call | solution.py:318
  267.8 11.3 %collective-permute-done.28 = bf16[16,64,256]{2,1,0:T(8,128)(2,1)S(1)} collective-permute-done((bf16[16,64,256]{2,1,0:T(8,128)(2,1)S(1)}, bf16[16,64,256]{2,1,0:T(8,128)(2,1)S(1)}, u32[]{:S(2)}, u32[]{:S(2)}) %collective-permute-start.28) | collective-permute-done | bytes 524320 | tf_op jit(solution)/shard_map/ppermute | solution.py:370
  280.3 4.7 all-to-all-start.4
  285.1 12.9 %all-to-all-done.4.packed_ref = bf16[16,64,384]{2,1,0:T(8,128)(2,1)S(1)} async-done(((bf16[16,64,384]{2,1,0:T(8,128)(2,1)}), bf16[16,64,384]{2,1,0:T(8,128)(2,1)S(1)}, u32[]{:S(2)}, u32[]{:S(2)}) %all-to-all-start.4) | async-done | bytes 786464 | tf_op jit(solution)/shard_map/all_to_all | solution.py:366
  307.5 6.6 %collective-permute-done.31 = bf16[128,1024]{1,0:T(8,128)(2,1)} collective-permute-done((bf16[128,1024]{1,0:T(8,128)(2,1)}, bf16[128,1024]{1,0:T(8,128)(2,1)}, u32[]{:S(2)}, u32[]{:S(2)}) %collective-permute-start.31) | collective-permute-done | bytes 262176 | tf_op jit(solution)/shard_map/ppermute | solution.py:343
  321.0 6.7 %all-to-all-start.5 = ((bf16[32,40,768]{2,1,0:T(8,128)(2,1)}), bf16[32,40,768]{2,1,0:T(8,128)(2,1)}, u32[]{:S(2)}, u32[]{:S(2)}) async-start(bf16[32,40,768]{2,1,0:T(8,128)(2,1)} %fusion.12), calls=%async_computation.5 | async-start | bytes 3932160 | tf_op jit(solution)/shard_map/all_to_all | solution.py:374
  337.3 19.9 %all-to-all-done.5 = bf16[32,40,768]{2,1,0:T(8,128)(2,1)} async-done(((bf16[32,40,768]{2,1,0:T(8,128)(2,1)}), bf16[32,40,768]{2,1,0:T(8,128)(2,1)}, u32[]{:S(2)}, u32[]{:S(2)}) %all-to-all-start.5) | async-done | bytes 1966112 | tf_op jit(solution)/shard_map/all_to_all | solution.py:374
  357.3 6.7 %all-to-all-start.6 = ((bf16[32,72,1024]{2,1,0:T(8,128)(2,1)}), bf16[32,72,1024]{2,1,0:T(8,128)(2,1)}, u32[]{:S(2)}, u32[]{:S(2)}) async-start(bf16[32,72,1024]{2,1,0:T(8,128)(2,1)} %pad_maximum_fusion), calls=%async_computation.6 | async-start | bytes 9437184 | tf_op jit(solution)/shard_map/all_to_all | solution.py:374
  369.5 13.5 %collective-permute-done.37 = bf16[128]{0:T(256)(128)(2,1)S(1)} collective-permute-done((bf16[128]{0:T(256)(128)(2,1)S(1)}, bf16[128]{0:T(256)(128)(2,1)S(1)}, u32[]{:S(2)}, u32[]{:S(2)}) %collective-permute-start.37) | collective-permute-done | bytes 288 | tf_op jit(solution)/shard_map/ppermute | solution.py:343
  385.1 51.7 %all-to-all-done.6 = bf16[32,72,1024]{2,1,0:T(8,128)(2,1)} async-done(((bf16[32,72,1024]{2,1,0:T(8,128)(2,1)}), bf16[32,72,1024]{2,1,0:T(8,128)(2,1)}, u32[]{:S(2)}, u32[]{:S(2)}) %all-to-all-start.6) | async-done | bytes 4718624 | tf_op jit(solution)/shard_map/all_to_all | solution.py:374
  445.9 42.8 %all-gather.7.cloned.1.call-done = bf16[1024,1024]{1,0:T(8,128)(2,1)} async-done(((bf16[32,1024]{1,0:T(8,128)(2,1)}), bf16[1024,1024]{1,0:T(8,128)(2,1)}) %all-gather.7.cloned.1.call-update) | async-done | bytes 2097168 | tf_op jit(solution)/shard_map/all_gather | solution.py:545
  494.9 79.3 %all-gather.9.cloned.1.call-done = bf16[2304,1024]{1,0:T(8,128)(2,1)} async-done(((bf16[72,1024]{1,0:T(8,128)(2,1)}), bf16[2304,1024]{1,0:T(8,128)(2,1)}) %all-gather.9.cloned.1.call-update) | async-done | bytes 4718608 | tf_op jit(solution)/shard_map/all_gather | solution.py:512
  576.3 5.0 fusion.69
  (314 shorter events, 132.5 us)
Async XLA Ops:
  7.2 34.6 %collective-permute-start.2 = (bf16[128,1024]{1,0:T(8,128)(2,1)}, bf16[128,1024]{1,0:T(8,128)(2,1)S(1)}, u32[]{:S(2)}, u32[]{:S(2)}) collective-permute-start(bf16[128,1024]{1,0:T(8,128)(2,1)} %bitcast.228), channel_id=1, source_target_pairs={{0,3},{1,2},{2,1},{3,0},{4,7},{5,6},{6,5},{7,4},{8,11},{9,10},{10,... | collective-permute-start | bytes 786440 | tf_op jit(solution)/shard_map/ppermute | solution.py:343
  8.7 33.5 %collective-permute-start.1 = (bf16[128,1024]{1,0:T(8,128)(2,1)}, bf16[128,1024]{1,0:T(8,128)(2,1)S(1)}, u32[]{:S(2)}, u32[]{:S(2)}) collective-permute-start(bf16[128,1024]{1,0:T(8,128)(2,1)} %bitcast.229), channel_id=1, source_target_pairs={{0,2},{1,3},{2,0},{3,1},{4,6},{5,7},{6,4},{7,5},{8,10},{9,11},{10,... | collective-permute-start | bytes 786440 | tf_op jit(solution)/shard_map/ppermute | solution.py:343
  9.4 32.8 %collective-permute-start = (bf16[128,1024]{1,0:T(8,128)(2,1)}, bf16[128,1024]{1,0:T(8,128)(2,1)S(1)}, u32[]{:S(2)}, u32[]{:S(2)}) collective-permute-start(bf16[128,1024]{1,0:T(8,128)(2,1)} %bitcast.230), channel_id=1, source_target_pairs={{0,1},{1,0},{2,3},{3,2},{4,5},{5,4},{6,7},{7,6},{8,9},{9,8},{10,11... | collective-permute-start | bytes 786440 | tf_op jit(solution)/shard_map/ppermute | solution.py:343
  14.5 29.0 %collective-permute-start.5 = (bf16[256,768]{0,1:T(8,128)(2,1)}, bf16[256,768]{0,1:T(8,128)(2,1)}, u32[]{:S(2)}, u32[]{:S(2)}) collective-permute-start(bf16[256,768]{0,1:T(8,128)(2,1)} %bitcast.15), channel_id=1, source_target_pairs={{0,3},{1,2},{2,1},{3,0},{4,7},{5,6},{6,5},{7,4},{8,11},{9,10},{10,... | collective-permute-start | bytes 1179656 | tf_op jit(solution)/shard_map/ppermute | solution.py:343
  15.9 27.5 %collective-permute-start.4 = (bf16[256,768]{0,1:T(8,128)(2,1)}, bf16[256,768]{0,1:T(8,128)(2,1)}, u32[]{:S(2)}, u32[]{:S(2)}) collective-permute-start(bf16[256,768]{0,1:T(8,128)(2,1)} %bitcast.13), channel_id=1, source_target_pairs={{0,2},{1,3},{2,0},{3,1},{4,6},{5,7},{6,4},{7,5},{8,10},{9,11},{10,... | collective-permute-start | bytes 1179656 | tf_op jit(solution)/shard_map/ppermute | solution.py:343
  48.7 22.2 %all-to-all-start.1 = ((bf16[16,64,384]{2,1,0:T(8,128)(2,1)}), bf16[16,64,384]{2,1,0:T(8,128)(2,1)S(1)}, u32[]{:S(2)}, u32[]{:S(2)}) async-start(bf16[16,64,384]{2,1,0:T(8,128)(2,1)} %copy-done.2), calls=%async_computation.1 | async-start | bytes 1572864 | tf_op jit(solution)/shard_map/all_to_all | solution.py:366
  71.7 20.9 %collective-permute-start.6 = (bf16[16,64,256]{2,1,0:T(8,128)(2,1)}, bf16[16,64,256]{2,1,0:T(8,128)(2,1)S(1)}, u32[]{:S(2)}, u32[]{:S(2)}) collective-permute-start(bf16[16,64,256]{2,1,0:T(8,128)(2,1)} %slice.295), channel_id=1, source_target_pairs={{0,4},{4,0},{8,12},{12,8},{16,20},{20,16},{24,28},{28,24},{32,36},... | collective-permute-start | bytes 1572872 | tf_op jit(solution)/shard_map/ppermute | solution.py:370
  76.3 13.8 %all-to-all-start = ((f32[32,8,128]{2,1,0:T(8,128)}), f32[32,8,128]{2,1,0:T(8,128)S(1)}, u32[]{:S(2)}, u32[]{:S(2)}) async-start(f32[32,8,128]{2,1,0:T(8,128)} %pad.13), calls=%async_computation | async-start | bytes 262144 | tf_op jit(solution)/shard_map/all_to_all | solution.py:419
  80.2 52.0 %collective-permute-start.21 = (bf16[128,1024]{1,0:T(8,128)(2,1)}, bf16[128,1024]{1,0:T(8,128)(2,1)}, u32[]{:S(2)}, u32[]{:S(2)}) collective-permute-start(bf16[128,1024]{1,0:T(8,128)(2,1)} %bitcast.247), channel_id=1, source_target_pairs={{0,3},{1,2},{2,1},{3,0},{4,7},{5,6},{6,5},{7,4},{8,11},{9,10},{10,... | collective-permute-start | bytes 786440 | tf_op jit(solution)/shard_map/ppermute | solution.py:343
  127.2 14.1 %collective-permute-start.15 = (bf16[256,1024]{1,0:T(8,128)(2,1)}, bf16[256,1024]{1,0:T(8,128)(2,1)}, u32[]{:S(2)}, u32[]{:S(2)}) collective-permute-start(bf16[256,1024]{1,0:T(8,128)(2,1)} %get-tuple-element.62), channel_id=1, source_target_pairs={{0,3},{1,2},{2,1},{3,0},{4,7},{5,6},{6,5},{7,4},{8,11},{9,10},{10,... | collective-permute-start | bytes 1572872 | tf_op jit(solution)/shard_map/ppermute | solution.py:343
  128.7 24.9 %collective-permute-start.14 = (bf16[256,1024]{1,0:T(8,128)(2,1)}, bf16[256,1024]{1,0:T(8,128)(2,1)}, u32[]{:S(2)}, u32[]{:S(2)}) collective-permute-start(bf16[256,1024]{1,0:T(8,128)(2,1)} %get-tuple-element.63), channel_id=1, source_target_pairs={{0,2},{1,3},{2,0},{3,1},{4,6},{5,7},{6,4},{7,5},{8,10},{9,11},{10,... | collective-permute-start | bytes 1572872 | tf_op jit(solution)/shard_map/ppermute | solution.py:343
  132.2 21.4 %collective-permute-start.13 = (bf16[256,1024]{1,0:T(8,128)(2,1)}, bf16[256,1024]{1,0:T(8,128)(2,1)S(1)}, u32[]{:S(2)}, u32[]{:S(2)}) collective-permute-start(bf16[256,1024]{1,0:T(8,128)(2,1)} %get-tuple-element.61), channel_id=1, source_target_pairs={{0,1},{1,0},{2,3},{3,2},{4,5},{5,4},{6,7},{7,6},{8,9},{9,8},{10,11... | collective-permute-start | bytes 1572872 | tf_op jit(solution)/shard_map/ppermute | solution.py:343
  133.9 24.2 %collective-permute-start.9 = (bf16[128,1024]{1,0:T(8,128)(2,1)S(1)}, bf16[128,1024]{1,0:T(8,128)(2,1)S(1)}, u32[]{:S(2)}, u32[]{:S(2)}) collective-permute-start(bf16[128,1024]{1,0:T(8,128)(2,1)S(1)} %get-tuple-element.86), channel_id=1, source_target_pairs={{0,3},{1,2},{2,1},{3,0},{4,7},{5,6},{6,5},{7,4},{8,11},{9,10},{10,... | collective-permute-start | bytes 786440 | tf_op jit(solution)/shard_map/ppermute | solution.py:343
  134.7 29.4 %collective-permute-start.8 = (bf16[128,1024]{1,0:T(8,128)(2,1)S(1)}, bf16[128,1024]{1,0:T(8,128)(2,1)S(1)}, u32[]{:S(2)}, u32[]{:S(2)}) collective-permute-start(bf16[128,1024]{1,0:T(8,128)(2,1)S(1)} %get-tuple-element.87), channel_id=1, source_target_pairs={{0,2},{1,3},{2,0},{3,1},{4,6},{5,7},{6,4},{7,5},{8,10},{9,11},{10,... | collective-permute-start | bytes 786440 | tf_op jit(solution)/shard_map/ppermute | solution.py:343
  141.3 22.8 %collective-permute-start.7 = (bf16[128,1024]{1,0:T(8,128)(2,1)S(1)}, bf16[128,1024]{1,0:T(8,128)(2,1)S(1)}, u32[]{:S(2)}, u32[]{:S(2)}) collective-permute-start(bf16[128,1024]{1,0:T(8,128)(2,1)S(1)} %get-tuple-element.85), channel_id=1, source_target_pairs={{0,1},{1,0},{2,3},{3,2},{4,5},{5,4},{6,7},{7,6},{8,9},{9,8},{10,11... | collective-permute-start | bytes 786440 | tf_op jit(solution)/shard_map/ppermute | solution.py:343
  165.4 13.7 %collective-permute-start.11 = (bf16[128,1024]{1,0:T(8,128)(2,1)S(1)}, bf16[128,1024]{1,0:T(8,128)(2,1)S(1)}, u32[]{:S(2)}, u32[]{:S(2)}) collective-permute-start(bf16[128,1024]{1,0:T(8,128)(2,1)S(1)} %add_convert_fusion.2), channel_id=1, source_target_pairs={{0,2},{1,3},{2,0},{3,1},{4,6},{5,7},{6,4},{7,5},{8,10},{9,11},{10,... | collective-permute-start | bytes 786440 | tf_op jit(solution)/shard_map/ppermute | solution.py:343
  185.4 14.0 %collective-permute-start.23 = (bf16[128,1024]{1,0:T(8,128)(2,1)S(1)}, bf16[128,1024]{1,0:T(8,128)(2,1)S(1)}, u32[]{:S(2)}, u32[]{:S(2)}) collective-permute-start(bf16[128,1024]{1,0:T(8,128)(2,1)S(1)} %get-tuple-element.81), channel_id=1, source_target_pairs={{0,2},{1,3},{2,0},{3,1},{4,6},{5,7},{6,4},{7,5},{8,10},{9,11},{10,... | collective-permute-start | bytes 786440 | tf_op jit(solution)/shard_map/ppermute | solution.py:343
  188.3 16.1 %collective-permute-start.18 = (bf16[128,1024]{1,0:T(8,128)(2,1)S(1)}, bf16[128,1024]{1,0:T(8,128)(2,1)S(1)}, u32[]{:S(2)}, u32[]{:S(2)}) collective-permute-start(bf16[128,1024]{1,0:T(8,128)(2,1)S(1)} %get-tuple-element.83), channel_id=1, source_target_pairs={{0,3},{1,2},{2,1},{3,0},{4,7},{5,6},{6,5},{7,4},{8,11},{9,10},{10,... | collective-permute-start | bytes 786440 | tf_op jit(solution)/shard_map/ppermute | solution.py:343
  189.2 21.1 %collective-permute-start.17 = (bf16[128,1024]{1,0:T(8,128)(2,1)S(1)}, bf16[128,1024]{1,0:T(8,128)(2,1)S(1)}, u32[]{:S(2)}, u32[]{:S(2)}) collective-permute-start(bf16[128,1024]{1,0:T(8,128)(2,1)S(1)} %get-tuple-element.84), channel_id=1, source_target_pairs={{0,2},{1,3},{2,0},{3,1},{4,6},{5,7},{6,4},{7,5},{8,10},{9,11},{10,... | collective-permute-start | bytes 786440 | tf_op jit(solution)/shard_map/ppermute | solution.py:343
  193.2 17.2 %collective-permute-start.16 = (bf16[128,1024]{1,0:T(8,128)(2,1)S(1)}, bf16[128,1024]{1,0:T(8,128)(2,1)S(1)}, u32[]{:S(2)}, u32[]{:S(2)}) collective-permute-start(bf16[128,1024]{1,0:T(8,128)(2,1)S(1)} %get-tuple-element.82), channel_id=1, source_target_pairs={{0,1},{1,0},{2,3},{3,2},{4,5},{5,4},{6,7},{7,6},{8,9},{9,8},{10,11... | collective-permute-start | bytes 786440 | tf_op jit(solution)/shard_map/ppermute | solution.py:343
  211.8 14.1 %collective-permute-start.26 = (bf16[128,1024]{1,0:T(8,128)(2,1)S(1)}, bf16[128,1024]{1,0:T(8,128)(2,1)S(1)}, u32[]{:S(2)}, u32[]{:S(2)}) collective-permute-start(bf16[128,1024]{1,0:T(8,128)(2,1)S(1)} %get-tuple-element.43), channel_id=1, source_target_pairs={{0,2},{1,3},{2,0},{3,1},{4,6},{5,7},{6,4},{7,5},{8,10},{9,11},{10,... | collective-permute-start | bytes 786440 | tf_op jit(solution)/shard_map/ppermute | solution.py:343
  265.1 14.0 %collective-permute-start.28 = (bf16[16,64,256]{2,1,0:T(8,128)(2,1)S(1)}, bf16[16,64,256]{2,1,0:T(8,128)(2,1)S(1)}, u32[]{:S(2)}, u32[]{:S(2)}) collective-permute-start(bf16[16,64,256]{2,1,0:T(8,128)(2,1)S(1)} %get-tuple-element.31), channel_id=1, source_target_pairs={{0,4},{4,0},{8,12},{12,8},{16,20},{20,16},{24,28},{28,24},{32,36},... | collective-permute-start | bytes 1572872 | tf_op jit(solution)/shard_map/ppermute | solution.py:370
  280.3 17.8 %all-to-all-start.4 = ((bf16[16,64,384]{2,1,0:T(8,128)(2,1)}), bf16[16,64,384]{2,1,0:T(8,128)(2,1)S(1)}, u32[]{:S(2)}, u32[]{:S(2)}) async-start(bf16[16,64,384]{2,1,0:T(8,128)(2,1)} %pad_maximum_fusion.8), calls=%async_computation.4 | async-start | bytes 1572864 | tf_op jit(solution)/shard_map/all_to_all | solution.py:366
  321.0 36.2 %all-to-all-start.5 = ((bf16[32,40,768]{2,1,0:T(8,128)(2,1)}), bf16[32,40,768]{2,1,0:T(8,128)(2,1)}, u32[]{:S(2)}, u32[]{:S(2)}) async-start(bf16[32,40,768]{2,1,0:T(8,128)(2,1)} %fusion.12), calls=%async_computation.5 | async-start | bytes 3932160 | tf_op jit(solution)/shard_map/all_to_all | solution.py:374
  357.3 79.5 %all-to-all-start.6 = ((bf16[32,72,1024]{2,1,0:T(8,128)(2,1)}), bf16[32,72,1024]{2,1,0:T(8,128)(2,1)}, u32[]{:S(2)}, u32[]{:S(2)}) async-start(bf16[32,72,1024]{2,1,0:T(8,128)(2,1)} %pad_maximum_fusion), calls=%async_computation.6 | async-start | bytes 9437184 | tf_op jit(solution)/shard_map/all_to_all | solution.py:374
  364.0 124.7 %all-gather.7.cloned.1.call-start = ((), (), s32[]{:S(2)}) async-start(), calls=%async_computation.7 | async-start | bytes 2162688 | tf_op jit(solution)/shard_map/all_gather | solution.py:545
  365.9 17.2 %collective-permute-start.37 = (bf16[128]{0:T(256)(128)(2,1)S(1)}, bf16[128]{0:T(256)(128)(2,1)S(1)}, u32[]{:S(2)}, u32[]{:S(2)}) collective-permute-start(bf16[128]{0:T(256)(128)(2,1)S(1)} %get-tuple-element.105), channel_id=1, source_target_pairs={{0,3},{1,2},{2,1},{3,0},{4,7},{5,6},{6,5},{7,4},{8,11},{9,10},{10,... | collective-permute-start | bytes 776 | tf_op jit(solution)/shard_map/ppermute | solution.py:343
  366.0 17.1 %collective-permute-start.36 = (bf16[128]{0:T(256)(128)(2,1)S(1)}, bf16[128]{0:T(256)(128)(2,1)S(1)}, u32[]{:S(2)}, u32[]{:S(2)}) collective-permute-start(bf16[128]{0:T(256)(128)(2,1)S(1)} %get-tuple-element.106), channel_id=1, source_target_pairs={{0,2},{1,3},{2,0},{3,1},{4,6},{5,7},{6,4},{7,5},{8,10},{9,11},{10,... | collective-permute-start | bytes 776 | tf_op jit(solution)/shard_map/ppermute | solution.py:343
  367.0 16.1 %collective-permute-start.35 = (bf16[128]{0:T(256)(128)(2,1)S(1)}, bf16[128]{0:T(256)(128)(2,1)S(1)}, u32[]{:S(2)}, u32[]{:S(2)}) collective-permute-start(bf16[128]{0:T(256)(128)(2,1)S(1)} %get-tuple-element.104), channel_id=1, source_target_pairs={{0,1},{1,0},{2,3},{3,2},{4,5},{5,4},{6,7},{7,6},{8,9},{9,8},{10,11... | collective-permute-start | bytes 776 | tf_op jit(solution)/shard_map/ppermute | solution.py:343
  367.8 15.3 %collective-permute-start.34 = (bf16[8,768]{1,0:T(8,128)(2,1)S(1)}, bf16[8,768]{1,0:T(8,128)(2,1)S(1)}, u32[]{:S(2)}, u32[]{:S(2)}) collective-permute-start(bf16[8,768]{1,0:T(8,128)(2,1)S(1)} %get-tuple-element.101), channel_id=1, source_target_pairs={{0,3},{1,2},{2,1},{3,0},{4,7},{5,6},{6,5},{7,4},{8,11},{9,10},{10,... | collective-permute-start | bytes 36872 | tf_op jit(solution)/shard_map/ppermute | solution.py:343
  368.2 15.0 %collective-permute-start.33 = (bf16[8,768]{1,0:T(8,128)(2,1)S(1)}, bf16[8,768]{1,0:T(8,128)(2,1)S(1)}, u32[]{:S(2)}, u32[]{:S(2)}) collective-permute-start(bf16[8,768]{1,0:T(8,128)(2,1)S(1)} %get-tuple-element.102), channel_id=1, source_target_pairs={{0,2},{1,3},{2,0},{3,1},{4,6},{5,7},{6,4},{7,5},{8,10},{9,11},{10,... | collective-permute-start | bytes 36872 | tf_op jit(solution)/shard_map/ppermute | solution.py:343
  385.0 189.2 %all-gather.9.cloned.1.call-start = ((), (), s32[]{:S(2)}) async-start(), calls=%async_computation.8 | async-start | bytes 4866048 | tf_op jit(solution)/shard_map/all_gather | solution.py:512
  (61 other events, 699.4 us)
Sparse Core Ops, SparseCore 0:
  385.1 103.5 all-gather.6
  492.2 81.9 all-gather.8
